TPU v7x, 128 devices: a whole 4x4x4 slice. The times are simulated.
128 devices in a mesh: ctx: 32 (over x, y, core), head: 4 (over z).
Axes of the slice: x: 4, y: 4, z: 4, core: 2. Of those that a mesh axis runs over, the one named last changes fastest.
Arguments:
- queries: bfloat16 [128, 4, 2048], P(None, 'head'), may hold values from -160 to 160, as said below
- key_codes: int32 [4, 128, 8, 32768], P('head', None, None, 'ctx'), may hold values from 0 to 255, as said below
- value_codes: int32 [4, 128, 8, 32768], P('head', None, None, 'ctx'), may hold values from 0 to 255
- key_book: bfloat16 [4, 8, 256, 16], P('head'), may hold values from -4 to 4
- value_book: bfloat16 [4, 8, 256, 16], P('head'), may hold values from -4 to 4
- lengths: int32 [128], replicated, may hold values from 1 to 32768, as said below
- resid: bfloat16 [128, 4096], P(None, 'ctx'), may hold values from -70 to 70
- w_out: bfloat16 [4, 2048, 4096], P('head', None, 'ctx'), may hold values from -2.5 to 2.5
- norm_gain: bfloat16 [4096], P('ctx'), may hold values from 0.25 to 1.75
- routes: int32 [128, 8], replicated, may hold values from 0 to 127, all different within a row; in each aligned block of 128 rows (0 to 127, 128 to 255, ...) at most 16 rows name the same one
- route_weights: float32 [128, 8], replicated, may hold values from 0.1 to 1
- w_gate: bfloat16 [128, 4096, 768], P(('ctx', 'head')), may hold values from -0.09375 to 0.09375
- w_up: bfloat16 [128, 4096, 768], P(('ctx', 'head')), may hold values from -0.09375 to 0.09375
- w_down: bfloat16 [128, 768, 4096], P(('ctx', 'head')), may hold values from -0.21875 to 0.21875
Outputs:
- layer_out: bfloat16 [128, 4096], P('head', 'ctx')
Inputs may be any that keep to these rules, and one draw needn't show every extreme that they name: `queries`: query rows of a few draws may be far larger than others. `key_codes`: at positions p with p mod 64 equal to 5 every code is 0; at p mod 64 equal to 9 subvector 0 has code 1 and the others 0. `lengths`: some row has length 32768. `routes`: each row names 8 different experts; no expert is named by more than 16 rows, and one is named by exactly 16; every expert is named by some row.
All inputs are finite; a program needn't handle non-finite values.
Results may differ from a plain program's by a relative error of at most 0.007.
Values may be sent and summed in bfloat16 or wider, within the bound.
A program may use at most 192 MiB of HBM per device.

v0:
```python
from functools import partial
import math

import jax
import jax.numpy as jnp
from jax import lax
from jax.sharding import PartitionSpec as P

masked_score = -1e30
epsilon = 1e-06


def dequantize(code_block, codebook):
    centers = lax.iota(jnp.int32, codebook.shape[1])
    onehot_codes = (code_block[:, :, None, :] == centers[None, None, :, None]).astype(jnp.bfloat16)
    vectors = jnp.einsum(
        "scd,rsct->rsdt", codebook, onehot_codes, preferred_element_type=jnp.float32
    )
    return vectors.astype(jnp.bfloat16).reshape(vectors.shape[0], -1, vectors.shape[3])


def attend_block(packed, key_table, value_table, offset):
    query_block, key_block, value_block, length_block = packed
    key_vectors = dequantize(key_block, key_table)
    value_vectors = dequantize(value_block, value_table)
    head_size = key_vectors.shape[1]
    scores = jnp.einsum(
        "rhk,rkt->rht", query_block, key_vectors, preferred_element_type=jnp.float32
    ) * (1.0 / math.sqrt(head_size))
    positions = offset + lax.iota(jnp.int32, key_vectors.shape[2])
    visible = positions[None, None, :] < length_block[:, None, None]
    maxima = jnp.max(jnp.where(visible, scores, masked_score), axis=-1)
    weights = jnp.exp(jnp.where(visible, scores - maxima[..., None], masked_score))
    totals = jnp.sum(weights, axis=-1)
    outputs = jnp.einsum(
        "rht,rkt->rhk",
        weights.astype(jnp.bfloat16),
        value_vectors,
        preferred_element_type=jnp.float32,
    )
    return (maxima, totals, outputs)


def on_device(
    queries,
    key_codes,
    value_codes,
    key_book,
    value_book,
    lengths,
    resid,
    w_out,
    norm_gain,
    routes,
    route_weights,
    w_gate,
    w_up,
    w_down,
):
    row_count = queries.shape[0]
    key_table = key_book[0]
    value_table = value_book[0]
    head_size = key_table.shape[0] * key_table.shape[2]
    head_count = queries.shape[2] // head_size
    slice_length = key_codes.shape[3]
    sub_count = key_codes.shape[2]
    block_rows = min(8, row_count)
    block_count = row_count // block_rows
    offset = lax.axis_index("ctx") * slice_length
    packed = (
        queries.reshape(block_count, block_rows, head_count, head_size),
        key_codes[0].reshape(block_count, block_rows, sub_count, slice_length),
        value_codes[0].reshape(block_count, block_rows, sub_count, slice_length),
        lengths.reshape(block_count, block_rows),
    )
    attend = partial(attend_block, key_table=key_table, value_table=value_table, offset=offset)
    maxima, totals, outputs = lax.map(attend, packed)
    maxima = maxima.reshape(row_count, head_count)
    totals = totals.reshape(row_count, head_count)
    outputs = outputs.reshape(row_count, head_count, head_size)
    highest = lax.pmax(maxima, "ctx")
    factors = jnp.exp(maxima - highest)
    totals, outputs = lax.psum((totals * factors, outputs * factors[..., None]), "ctx")
    attended = (
        (outputs / totals[..., None])
        .astype(jnp.bfloat16)
        .reshape(row_count, head_count * head_size)
    )
    partial_proj = jnp.dot(attended, w_out[0], preferred_element_type=jnp.float32)
    projected = lax.psum(partial_proj, "head")
    residual = (resid.astype(jnp.float32) + projected).astype(jnp.bfloat16)
    ctx_count = lax.axis_size("ctx")
    head_axis = lax.axis_size("head")
    width = resid.shape[1] * ctx_count
    local_rows = residual.astype(jnp.float32)
    square_sums = lax.psum(jnp.sum(local_rows * local_rows, axis=1), "ctx")
    scaled = (
        local_rows
        * lax.rsqrt(square_sums / width + epsilon)[:, None]
        * norm_gain.astype(jnp.float32)[None, :]
    )
    normed_full = lax.all_gather(scaled.astype(jnp.bfloat16), "ctx", axis=1, tiled=True)
    expert_total = ctx_count * head_axis
    expert_id = lax.axis_index(("ctx", "head"))
    capacity = 16 * row_count // expert_total
    chosen = routes == expert_id
    routed = jnp.any(chosen, axis=1)
    weight_col = jnp.sum(jnp.where(chosen, route_weights, 0.0), axis=1)
    slot_index = jnp.cumsum(routed.astype(jnp.int32)) - 1
    slots = lax.iota(jnp.int32, capacity)[:, None]
    selector = ((slot_index[None, :] == slots) & routed[None, :]).astype(jnp.bfloat16)
    taken_rows = jnp.dot(selector, normed_full, preferred_element_type=jnp.float32).astype(
        jnp.bfloat16
    )
    gate_act = jnp.dot(taken_rows, w_gate[0], preferred_element_type=jnp.float32)
    up_act = jnp.dot(taken_rows, w_up[0], preferred_element_type=jnp.float32)
    hidden = (jax.nn.silu(gate_act) * up_act).astype(jnp.bfloat16)
    expert_out = jnp.dot(hidden, w_down[0], preferred_element_type=jnp.float32).astype(jnp.bfloat16)
    share_rows = row_count // head_axis
    share_cols = width // ctx_count
    placer = selector.T.reshape(head_axis, share_rows, capacity)
    spread = jnp.einsum(
        "hrk,kcd->chrd",
        placer,
        expert_out.reshape(capacity, ctx_count, share_cols),
        preferred_element_type=jnp.float32,
    )
    spread = spread * weight_col.reshape(1, head_axis, share_rows, 1)
    mixture = lax.psum_scatter(
        spread.reshape(ctx_count * head_axis * share_rows, share_cols),
        ("ctx", "head"),
        scatter_dimension=0,
        tiled=True,
    )
    own_rows = lax.dynamic_slice_in_dim(
        residual, lax.axis_index("head") * share_rows, share_rows, 0
    )
    return (own_rows.astype(jnp.float32) + mixture).astype(jnp.bfloat16)


def solution(mesh):
    return jax.shard_map(
        on_device,
        mesh=mesh,
        in_specs=(
            P(None, "head", None),
            P("head", None, None, "ctx"),
            P("head", None, None, "ctx"),
            P("head", None, None, None),
            P("head", None, None, None),
            P(),
            P(None, "ctx"),
            P("head", None, "ctx"),
            P("ctx"),
            P(),
            P(),
            P(("ctx", "head"), None, None),
            P(("ctx", "head"), None, None),
            P(("ctx", "head"), None, None),
        ),
        out_specs=P("head", "ctx"),
        check_vma=False,
    )
```

profile of v0, /device:TPU:1, one launch (start us, length us, event | category | flops | bytes accessed | tf_op | source)
XLA Modules:
  0.0 1511.7 jit_solution(4501459408046640463)
XLA Ops:
  6.5 1.2 copy.42
  8.5 448.2 %while.14 = (s32[]{:T(128)}, f32[16,8,16]{2,1,0:T(8,128)S(1)}, f32[16,8,16]{2,1,0:T(8,128)S(1)}, f32[16,8,16,128]{3,2,1,0:T(8,128)S(1)}, s32[]{:T(128)}, /*index...) while((s32[]{:T(128)}, f32[16,8,16]{2,1,0:T(8,128)S(1)}, ...), condition=%wide.region_3.4_spmd, body=%wide.region_0.3_spmd.sunk | while | flops 1177690880 | bytes 21526284 | solution.py:77
  8.6 1.0 constant_dynamic-slice_fusion.5
  9.7 12.3 convert_bitcast_fusion.5
  22.7 1.0 constant_dynamic-slice_fusion.6
  23.9 11.4 convert_bitcast_fusion.6
  37.7 12.3 convert_bitcast_fusion.5
  50.8 1.0 constant_dynamic-slice_fusion.6
  51.9 11.4 convert_bitcast_fusion.6
  65.8 12.3 convert_bitcast_fusion.5
  78.8 1.0 constant_dynamic-slice_fusion.6
  79.9 11.4 convert_bitcast_fusion.6
  93.8 12.3 convert_bitcast_fusion.5
  106.8 1.0 constant_dynamic-slice_fusion.6
  107.9 11.4 convert_bitcast_fusion.6
  121.8 12.3 convert_bitcast_fusion.5
  134.8 1.0 constant_dynamic-slice_fusion.6
  136.0 11.4 convert_bitcast_fusion.6
  149.8 12.3 convert_bitcast_fusion.5
  162.8 1.0 constant_dynamic-slice_fusion.6
  164.0 11.4 convert_bitcast_fusion.6
  177.8 12.3 convert_bitcast_fusion.5
  190.8 1.0 constant_dynamic-slice_fusion.6
  192.0 11.4 convert_bitcast_fusion.6
  205.8 12.3 convert_bitcast_fusion.5
  218.9 1.0 constant_dynamic-slice_fusion.6
  220.0 11.4 convert_bitcast_fusion.6
  233.9 12.3 convert_bitcast_fusion.5
  246.9 1.0 constant_dynamic-slice_fusion.6
  248.0 11.4 convert_bitcast_fusion.6
  261.9 12.3 convert_bitcast_fusion.5
  274.9 1.0 constant_dynamic-slice_fusion.6
  276.0 11.4 convert_bitcast_fusion.6
  289.9 12.3 convert_bitcast_fusion.5
  302.9 1.0 constant_dynamic-slice_fusion.6
  304.1 11.4 convert_bitcast_fusion.6
  317.9 12.3 convert_bitcast_fusion.5
  330.9 1.0 constant_dynamic-slice_fusion.6
  332.1 11.4 convert_bitcast_fusion.6
  345.9 12.3 convert_bitcast_fusion.5
  358.9 1.0 constant_dynamic-slice_fusion.6
  360.1 11.4 convert_bitcast_fusion.6
  373.9 12.3 convert_bitcast_fusion.5
  386.9 1.0 constant_dynamic-slice_fusion.6
  388.1 11.4 convert_bitcast_fusion.6
  402.0 12.3 convert_bitcast_fusion.5
  415.0 1.0 constant_dynamic-slice_fusion.6
  416.1 11.4 convert_bitcast_fusion.6
  430.0 12.3 convert_bitcast_fusion.5
  443.0 1.0 constant_dynamic-slice_fusion.6
  444.1 11.4 convert_bitcast_fusion.6
  456.8 124.4 %pmax.7 = f32[128,16]{1,0:T(8,128)S(1)} all-reduce(f32[128,16]{1,0:T(8,128)S(1)} %bitcast.140), channel_id=1, replica_groups=mesh['ctx'=32,'head'=4] {'ctx'}, use_global_device_ids=true, to_apply=%region_4.5 | all-reduce | flops 2048 | bytes 16384 | tf_op jit(solution)/shard_map/pmax | solution.py:81
  581.2 1.4 bitcast_multiply_fusion
  582.6 123.9 %psum.29 = f32[128,16]{1,0:T(8,128)S(1)} all-reduce(f32[128,16]{1,0:T(8,128)S(1)} %get-tuple-element.104), channel_id=1, replica_groups=mesh['ctx'=32,'head'=4] {'ctx'}, use_global_device_ids=true, to_apply=%region_6.7 | all-reduce | flops 2048 | bytes 16384 | tf_op jit(solution)/shard_map/psum | solution.py:83
  706.5 1.6 divide_convert_fusion
  709.1 41.5 %all-reduce.5.cloned.1.call-done = f32[128,128]{1,0:T(8,128)} async-done(((f32[128,128]{1,0:T(8,128)}), f32[128,128]{1,0:T(8,128)}) %all-reduce.5.cloned.1.call-update) | async-done | bytes 65552 | tf_op jit(solution)/shard_map/psum | solution.py:90
  751.6 64.7 %psum.31 = f32[128]{0:T(128)S(1)} all-reduce(f32[128]{0:T(128)S(1)} %get-tuple-element.102), channel_id=1, replica_groups=mesh['ctx'=32,'head'=4] {'ctx'}, use_global_device_ids=true, to_apply=%region_11.12 | all-reduce | flops 128 | bytes 1024 | tf_op jit(solution)/shard_map/psum | solution.py:96
  817.9 40.4 %all-gather.2.cloned.1.call-done = bf16[128,4096]{1,0:T(8,128)(2,1)} async-done(((bf16[128,128]{1,0:T(8,128)(2,1)}), bf16[128,4096]{1,0:T(8,128)(2,1)}) %all-gather.2.cloned.1.call-update) | async-done | bytes 1048592 | tf_op jit(solution)/shard_map/all_gather | solution.py:102
  858.3 1.5 convolution_convert_fusion
  859.8 3.7 fusion.22
  863.5 7.0 fusion.27
  870.5 1.8 convolution_multiply_fusion.1
  872.4 631.5 %reduce-scatter.2.cloned.1.call-done = f32[32,128]{1,0:T(8,128)} async-done(((f32[4096,128]{1,0:T(8,128)}), f32[32,128]{1,0:T(8,128)}) %reduce-scatter.2.cloned.1.call-update) | async-done | bytes 16400 | tf_op jit(solution)/shard_map/reduce_scatter | solution.py:129
  1503.9 1.3 add_convert_fusion.1
  (261 shorter events, 55.3 us)
Async XLA Ops:
  6.5 701.6 %copy-start = (bf16[1,2048,128]{2,1,0:T(8,128)(2,1)S(1)}, bf16[1,2048,128]{2,1,0:T(8,128)(2,1)}, u32[]{:S(2)}) copy-start(bf16[1,2048,128]{2,1,0:T(8,128)(2,1)} %param.23) | copy-start | bytes 1572868
  6.5 700.0 %all-reduce.3.cloned.1.call-start = ((), (), s32[]{:S(2)}) async-start(), calls=%async_computation.1 | async-start | bytes 2097152 | tf_op jit(solution)/shard_map/psum | solution.py:83
  22.0 1.9 copy-start.4
  50.0 1.9 copy-start.4
  78.0 1.9 copy-start.4
  106.1 1.9 copy-start.4
  134.1 1.9 copy-start.4
  162.1 1.9 copy-start.4
  190.1 1.9 copy-start.4
  218.1 1.9 copy-start.4
  246.1 1.9 copy-start.4
  274.1 1.9 copy-start.4
  302.2 1.9 copy-start.4
  330.2 1.9 copy-start.4
  358.2 1.9 copy-start.4
  386.2 1.9 copy-start.4
  414.2 1.9 copy-start.4
  442.2 1.9 copy-start.4
  456.7 252.4 %copy-start.5 = (bf16[128]{0:T(256)(128)(2,1)S(1)}, bf16[128]{0:T(256)(128)(2,1)}, u32[]{:S(2)}) copy-start(bf16[128]{0:T(256)(128)(2,1)} %param.24) | copy-start | bytes 772
  456.7 293.9 %copy-start.1 = (bf16[128,128]{1,0:T(8,128)(2,1)S(1)}, bf16[128,128]{1,0:T(8,128)(2,1)}, u32[]{:S(2)}) copy-start(bf16[128,128]{1,0:T(8,128)(2,1)} %param.22) | copy-start | bytes 98308
  456.8 360.5 %copy-start.2 = (s32[128,8]{0,1:T(8,128)S(1)}, s32[128,8]{0,1:T(8,128)}, u32[]{:S(2)}) copy-start(s32[128,8]{0,1:T(8,128)} %param.25) | copy-start | bytes 12292
  456.8 361.0 %copy-start.3 = (f32[128,8]{0,1:T(8,128)S(1)}, f32[128,8]{0,1:T(8,128)}, u32[]{:S(2)}) copy-start(f32[128,8]{0,1:T(8,128)} %param.26) | copy-start | bytes 12292
  582.6 168.1 %all-reduce.5.cloned.1.call-start = ((), (), s32[]{:S(2)}) async-start(), calls=%async_computation.2 | async-start | bytes 131072 | tf_op jit(solution)/shard_map/psum | solution.py:90
  709.1 149.3 %all-gather.2.cloned.1.call-start = ((), (), s32[]{:S(2)}) async-start(), calls=%async_computation.3 | async-start | bytes 1081344 | tf_op jit(solution)/shard_map/all_gather | solution.py:102
  817.0 686.8 %reduce-scatter.2.cloned.1.call-start = ((), (), s32[]{:S(2)}) async-start(), calls=%async_computation.4 | async-start | bytes 2113536 | tf_op jit(solution)/shard_map/reduce_scatter | solution.py:129
Sparse Core Ops, SparseCore 0:
  582.7 106.8 all-reduce.2
  709.2 41.4 all-reduce.4
  817.1 41.1 all-gather.1
  872.5 631.3 reduce-scatter.1
where the time goes:
time: 1520 us; the launch traced here: 1510 us
  waiting for transfers between devices  713 us (47%)
  matrix products  413 us (27%)
  blocking collectives  313 us (21%)
  local copies, waits for them, and re-layouts  45.9 us (3%)
    reduce_scatter x1, waiting for transfers between devices, on_device(): lax.psum_scatter(spread.reshape(ctx_count * head_axis * share_rows, share...  631 us
    dot_general x32, matrix products, dequantize(): jnp.einsum('scd,rsct->rsdt', codebook, onehot_codes, preferred_element_ty...  379 us
    pmax x1, blocking collectives, on_device(): highest = lax.pmax(maxima, 'ctx')  124 us
    psum x1, blocking collectives, on_device(): lax.psum((totals * factors, outputs * factors[..., None]), 'ctx')  124 us
    psum x1, blocking collectives, on_device(): square_sums = lax.psum(jnp.sum(local_rows * local_rows, axis=1), 'ctx')  64.7 us
    psum x1, waiting for transfers between devices, on_device(): projected = lax.psum(partial_proj, 'head')  41.5 us
    all_gather x1, waiting for transfers between devices, on_device(): lax.all_gather(scaled.astype(jnp.bfloat16), 'ctx', axis=1, tiled=True)  40.4 us
    dynamic_slice x64, local copies, waits for them, and re-layouts, on_device(): maxima, totals, outputs = lax.map(attend, packed)  36.1 us
  transfers between devices with their start and end apart: 4, of which 3 were waited for; matrix products, arithmetic and copies ran while one was open for 0% of the time, Pallas kernels for 0%

commit v1 on v0

v1 whole, which is shorter than its diff:
```python
import functools, math
import jax, jax.numpy as jnp
from jax import lax
from jax.experimental import pallas as pl
from jax.experimental.pallas import tpu as pltpu
from jax.sharding import PartitionSpec as P
LOG2E = 1.4426950408889634
f32, bf16, i32 = jnp.float32, jnp.bfloat16, jnp.int32
ROWS, CH, CAP, N_CTX, N_HEAD = 128, 16, 16, 32, 4
MESH = pl.DeviceIdType.MESH

def pow2_scale(x):
    sc = jnp.ones_like(x)
    for p in (32, 16, 8, 4, 2, 1):
        f = float(2.0 ** p)
        ok = x * f <= 4.0
        x = jnp.where(ok, x * f, x)
        sc = jnp.where(ok, sc * f, sc)
    return sc

def build_table(book_ref, table_ref):
    top = jnp.zeros((8, 256), f32)
    for d in range(16):
        top = jnp.maximum(top, jnp.abs(book_ref[d].astype(f32)))
    sc = pow2_scale(jnp.max(top, axis=1, keepdims=True))
    for p in range(8):
        hi = jnp.round(book_ref[2 * p].astype(f32) * (sc * 4096.0)).astype(i32)
        lo = jnp.round(book_ref[2 * p + 1].astype(f32) * (sc * 4096.0)).astype(i32)
        word = hi * 65536 + lo
        table_ref[2 * p] = word[:, :128]
        table_ref[2 * p + 1] = word[:, 128:]
    inv = 1.0 / sc * (2.0 ** -28)
    lane = lax.broadcasted_iota(i32, (8, 128), 1)
    sub = lax.broadcasted_iota(i32, (8, 128), 0)
    return jnp.sum(jnp.where(lane % 8 == sub, inv, 0.0), axis=0, keepdims=True)

def attn_kernel(len_ref, q_ref, kb_ref, vb_ref, gain_ref, kc_hbm, vc_hbm,
                o_ref, kc_ref, vc_ref, kt_ref, vt_ref, qp_ref, ox_ref, key_ref, val_ref, ml_ref, ksem, vsem, *, unroll, SL):
    def code_copy(c, hbm, vmem, sem):
        at = pl.ds(c * CH, CH)
        return pltpu.make_async_copy(hbm.at[0, at], vmem.at[at], sem.at[c])
    for c in range(ROWS // CH):
        code_copy(c, kc_hbm, kc_ref, ksem).start()
        code_copy(c, vc_hbm, vc_ref, vsem).start()
    offset = lax.axis_index("ctx") * 1024
    k_inv = build_table(kb_ref, kt_ref)
    v_inv = build_table(vb_ref, vt_ref)
    i = lax.broadcasted_iota(i32, (128, 128), 0)
    j = lax.broadcasted_iota(i32, (128, 128), 1)
    to_ds = (i // 16 == j % 8) & (i % 16 == j // 8)
    to_sd = (j // 16 == i % 8) & (j % 16 == i // 8)
    qp_ref[...] = jnp.dot(q_ref[...], jnp.where(to_ds, k_inv, 0.0).astype(bf16), preferred_element_type=f32).astype(bf16)
    ml_ref[...] = jnp.zeros_like(ml_ref)
    lane = lax.broadcasted_iota(i32, (16, 128), 1)
    pos = lax.broadcasted_iota(i32, (16, 1024), 1)
    C = 1.0 / math.sqrt(128.0)

    def dequant(codes_ref, b, table_ref, dst_ref, slot):
        for j in range(8):
            at = slice(j * 128, (j + 1) * 128)
            idx = codes_ref[b, :, at]
            low = idx & 127
            upper = idx > 127
            for p in range(8):
                w0 = jnp.take_along_axis(table_ref[2 * p], low, axis=1, mode="promise_in_bounds")
                w1 = jnp.take_along_axis(table_ref[2 * p + 1], low, axis=1, mode="promise_in_bounds")
                w = jnp.where(upper, w1, w0)
                pair = jnp.concatenate([w.astype(f32), (w << 16).astype(f32)], axis=0)
                dst_ref[slot, p * 16:(p + 1) * 16, at] = pair.astype(bf16)

    def fetch(b, slot):
        dequant(kc_ref, b, kt_ref, key_ref, slot)
        dequant(vc_ref, b, vt_ref, val_ref, slot)

    def row(b, slot):
        at = pl.ds(pl.multiple_of(b * 16, 16), 16)
        raw = jnp.dot(qp_ref[at, :], key_ref[slot], preferred_element_type=f32)
        vis = pos < len_ref[b] - offset
        raw = jnp.where(vis, raw, -1e30)
        top = jnp.max(raw, axis=1, keepdims=True)
        w = jnp.where(vis, jnp.exp2((raw - top) * (C * LOG2E)), 0.0)
        tot = jnp.sum(w, axis=1, keepdims=True)
        out = lax.dot_general(w.astype(bf16), val_ref[slot], (((1,), (1,)), ((), ())), preferred_element_type=f32)
        ox_ref[at, :] = (out * v_inv).astype(bf16)
        here = lane == b
        ml_ref[0] = jnp.where(here, top * C, ml_ref[0])
        ml_ref[1] = jnp.where(here, tot, ml_ref[1])

    def wait_chunk(c):
        code_copy(c, kc_hbm, kc_ref, ksem).wait()
        code_copy(c, vc_hbm, vc_ref, vsem).wait()
    wait_chunk(0)
    fetch(0, 0)

    def chunk(c, _):
        @pl.when(c < ROWS // CH - 1)
        def _():
            wait_chunk(c + 1)
        def body(i, _):
            b = c * CH + i * unroll
            for u in range(unroll):
                fetch(jnp.minimum(b + u + 1, ROWS - 1), (u + 1) % SL)
                row(b + u, u % SL)
            return 0
        lax.fori_loop(0, CH // unroll, body, 0)
        return 0
    lax.fori_loop(0, ROWS // CH, chunk, 0)
    r = lax.broadcasted_iota(i32, (256, 256), 0)
    c = lax.broadcasted_iota(i32, (256, 256), 1)
    swap = ((r // 16 == c % 16) & (r % 16 == c // 16)).astype(f32).astype(bf16)
    perm = jnp.where(to_sd, 1.0, 0.0).astype(bf16)
    for g in range(8):
        y = jnp.dot(swap, ox_ref[g * 256:(g + 1) * 256], preferred_element_type=f32).astype(bf16)
        y = jnp.dot(y, perm, preferred_element_type=f32).astype(bf16)
        for h in range(16):
            o_ref[h * 2 + g // 4, g % 4 * 16:g % 4 * 16 + 16, :] = y[h * 16:(h + 1) * 16]

    def three(x):
        hi = x.astype(bf16).astype(f32)
        mid = (x - hi).astype(bf16).astype(f32)
        return hi, mid, x - hi - mid
    pieces = three(ml_ref[0]) + three(ml_ref[1])
    line = lax.broadcasted_iota(i32, (16, 128), 0)
    gain = jnp.where(line == 6, gain_ref[...].astype(f32), 0.0)
    for h in range(16):
        tail = gain
        for k in range(6):
            tail = jnp.where(line == k, pieces[k][h:h + 1, :], tail)
        o_ref[2 * h, 64:80, :] = tail.astype(bf16)
        o_ref[2 * h + 1, 64:80, :] = tail.astype(bf16)

def attend(queries, key_codes, value_codes, key_book, value_book, lengths, norm_gain, unroll=4, SL=2):
    vm = pl.BlockSpec(memory_space=pltpu.VMEM)
    hbm = pl.BlockSpec(memory_space=pl.ANY)
    return pl.pallas_call(
        functools.partial(attn_kernel, unroll=unroll, SL=SL),
        in_specs=[pl.BlockSpec(memory_space=pltpu.SMEM), vm, vm, vm, vm, hbm, hbm],
        out_specs=vm,
        out_shape=jax.ShapeDtypeStruct((N_CTX, 80, 128), bf16),
        scratch_shapes=[pltpu.VMEM((ROWS, 8, 1024), i32), pltpu.VMEM((ROWS, 8, 1024), i32),
                        pltpu.VMEM((16, 8, 128), i32), pltpu.VMEM((16, 8, 128), i32),
                        pltpu.VMEM((2048, 128), bf16), pltpu.VMEM((2048, 128), bf16),
                        pltpu.VMEM((SL, 128, 1024), bf16), pltpu.VMEM((SL, 128, 1024), bf16),
                        pltpu.VMEM((2, 16, 128), f32),
                        pltpu.SemaphoreType.DMA((8,)), pltpu.SemaphoreType.DMA((8,))],
        compiler_params=pltpu.CompilerParams(vmem_limit_bytes=56 << 20),
    )(lengths, queries.reshape(2048, 128), jnp.transpose(key_book[0], (2, 0, 1)),
      jnp.transpose(value_book[0], (2, 0, 1)), norm_gain.reshape(1, 128), key_codes, value_codes)


def rest_kernel(msg_ref, resid_ref, wout_hbm, routes_ref, rw_ref, wg_hbm, wu_hbm, wd_hbm,
                out_ref,
                wout_ref, wg_ref, wu_ref, wd_ref, got_ref, att_ref, zsum_ref, take_ref, taken_ref, xn_ref,
                eo_ref, eogot_ref, part_ref, partgot_ref, gt_ref, sel_ref, selw_ref, wt_ref, res_ref,
                load_sem, send_sem, recv_sem):
    ctx = lax.axis_index("ctx")
    head = lax.axis_index("head")
    loads = [pltpu.make_async_copy(wout_hbm.at[0], wout_ref, load_sem.at[0]),
             pltpu.make_async_copy(wg_hbm.at[0], wg_ref, load_sem.at[1]),
             pltpu.make_async_copy(wu_hbm.at[0], wu_ref, load_sem.at[2]),
             pltpu.make_async_copy(wd_hbm.at[0], wd_ref, load_sem.at[3])]
    barrier = pltpu.get_barrier_semaphore()

    def greet_ctx(k, _):
        pl.semaphore_signal(barrier, inc=1, device_id={"ctx": lax.rem(ctx + k, N_CTX)}, device_id_type=MESH)
        return 0
    lax.fori_loop(1, N_CTX, greet_ctx, 0)
    for k in range(1, N_HEAD):
        pl.semaphore_signal(barrier, inc=1, device_id={"head": lax.rem(head + k, N_HEAD)}, device_id_type=MESH)
    pl.semaphore_wait(barrier, N_CTX - 1 + N_HEAD - 1)

    def send_all(phase, source, target):
        def step(k, _):
            to = lax.rem(ctx + k, N_CTX)
            pltpu.make_async_remote_copy(
                src_ref=source(to), dst_ref=target, send_sem=send_sem.at[phase], recv_sem=recv_sem.at[phase],
                device_id={"ctx": to}, device_id_type=MESH).start()
            return 0
        lax.fori_loop(1, N_CTX, step, 0)

    def wait_all(sems, phase, ref, count):
        view = ref.at[pl.ds(0, count)]
        pltpu.make_async_copy(view, view, sems.at[phase]).wait()

    send_all(0, lambda to: msg_ref.at[to], got_ref.at[ctx])
    for load in loads:
        load.start()
    got_ref[ctx] = msg_ref[ctx]

    eye = (lax.broadcasted_iota(i32, (8, 8), 0) == lax.broadcasted_iota(i32, (8, 8), 1)).astype(f32).astype(bf16)
    flip = lambda x: lax.dot_general(eye, x, (((1,), (1,)), ((), ())), preferred_element_type=f32)
    names = flip(routes_ref[...].astype(f32).astype(bf16)).astype(i32)
    rw = rw_ref[...]
    rw_hi = rw.astype(bf16)
    rw_mid = (rw - rw_hi.astype(f32)).astype(bf16)
    rw_lo = (rw - rw_hi.astype(f32) - rw_mid.astype(f32)).astype(bf16)
    shares = flip(rw_hi) + flip(rw_mid) + flip(rw_lo)
    expert = lax.broadcasted_iota(i32, (N_CTX, ROWS), 0) * N_HEAD + head
    member = jnp.zeros((N_CTX, ROWS), f32)
    weight = jnp.zeros((N_CTX, ROWS), f32)
    for k in range(8):
        same = names[k:k + 1, :] == expert
        member = jnp.where(same, 1.0, member)
        weight = jnp.where(same, shares[k:k + 1, :], weight)
    before = (lax.broadcasted_iota(i32, (ROWS, ROWS), 0) < lax.broadcasted_iota(i32, (ROWS, ROWS), 1)).astype(f32).astype(bf16)
    slot = jnp.dot(member.astype(bf16), before, preferred_element_type=f32).astype(i32)
    slot = jnp.where(member > 0.5, slot, -1)
    slots = lax.broadcasted_iota(i32, (CAP, ROWS), 0)
    for e in range(N_CTX):
        hit = slot[e:e + 1, :] == slots
        sel_ref[e * CAP:(e + 1) * CAP, :] = jnp.where(hit, 1.0, 0.0).astype(bf16)
        selw_ref[e * CAP:(e + 1) * CAP, :] = jnp.where(hit, weight[e:e + 1, :], 0.0)
    for t in range(N_CTX * CAP // 128):
        block = selw_ref[t * 128:(t + 1) * 128, :].T
        hi = block.astype(bf16)
        rest = block - hi.astype(f32)
        mid = rest.astype(bf16)
        wt_ref[0, :, t * 128:(t + 1) * 128] = hi
        wt_ref[1, :, t * 128:(t + 1) * 128] = mid
        wt_ref[2, :, t * 128:(t + 1) * 128] = (rest - mid.astype(f32)).astype(bf16)

    wait_all(recv_sem, 0, got_ref, N_CTX - 1)
    tails = got_ref[:, 64:80, :].reshape(N_CTX * 16, 128)
    r = lax.broadcasted_iota(i32, (3 * N_CTX, N_CTX * 16), 0)
    c = lax.broadcasted_iota(i32, (3 * N_CTX, N_CTX * 16), 1)
    kind, at = r // N_CTX, c % 16
    wanted = (c // 16 == r % N_CTX) & (at // 3 == kind) & (at < 7)
    stats = jnp.dot(jnp.where(wanted, 1.0, 0.0).astype(bf16), tails, preferred_element_type=f32)
    maxima, totals, gain = stats[:N_CTX], stats[N_CTX:2 * N_CTX], stats[2 * N_CTX:]
    factor = jnp.exp(maxima - jnp.max(maxima, axis=0, keepdims=True))
    factor = factor / jnp.sum(factor * totals, axis=0, keepdims=True)
    gt_ref[...] = jnp.concatenate([factor, jnp.zeros((ROWS - N_CTX, ROWS), f32)], axis=0).T
    mine = gt_ref[pl.ds(pl.multiple_of(lax.rem(ctx, 2) * 64, 64), 64), :]
    total = jnp.zeros((64, 128), f32)
    for s in range(N_CTX):
        total += mine[:, s:s + 1] * got_ref[s, :64, :].astype(f32)
    att_ref[ctx] = total.astype(bf16)
    send_all(1, lambda to: att_ref.at[ctx], att_ref.at[ctx])
    loads[0].wait()
    wait_all(recv_sem, 1, att_ref, N_CTX - 1)
    proj = jnp.zeros((ROWS, 128), f32)
    for h in range(16):
        rows = att_ref[2 * h:2 * h + 2].reshape(ROWS, 128)
        proj += jnp.dot(rows, wout_ref[h * 128:(h + 1) * 128, :], preferred_element_type=f32)

    def send_heads(phase, source, target):
        for k in range(1, N_HEAD):
            to = lax.rem(head + k, N_HEAD)
            pltpu.make_async_remote_copy(
                src_ref=source(to), dst_ref=target, send_sem=send_sem.at[phase], recv_sem=recv_sem.at[phase],
                device_id={"head": to}, device_id_type=MESH).start()

    zsum_ref[head] = proj
    send_heads(2, lambda to: zsum_ref.at[head], zsum_ref.at[head])
    wait_all(recv_sem, 2, zsum_ref, N_HEAD - 1)
    projected = (zsum_ref[0] + zsum_ref[1]) + (zsum_ref[2] + zsum_ref[3])
    residual = (resid_ref[...].astype(f32) + projected).astype(bf16)
    res_ref[...] = residual.astype(f32)

    take_ref[...] = jnp.dot(sel_ref[...], residual, preferred_element_type=f32).astype(bf16).reshape(N_CTX, CAP, 128)
    send_all(3, lambda to: take_ref.at[to], taken_ref.at[ctx])
    taken_ref[ctx] = take_ref[ctx]
    loads[1].wait()
    loads[2].wait()
    loads[3].wait()
    wait_all(recv_sem, 3, taken_ref, N_CTX - 1)
    squares = jnp.zeros((CAP, 128), f32)
    for s in range(N_CTX):
        piece = taken_ref[s].astype(f32)
        squares += piece * piece
    scale = lax.rsqrt(jnp.sum(squares, axis=1, keepdims=True) * (1.0 / 4096) + 1e-6)
    for s in range(N_CTX):
        piece = taken_ref[s].astype(f32) * scale * gain[s:s + 1, :]
        xn_ref[s // 4, :, s % 4 * 128:s % 4 * 128 + 128] = piece.astype(bf16)

    def up_step(k, acc):
        rows = pl.ds(pl.multiple_of(k * 512, 512), 512)
        x = xn_ref[k]
        return (acc[0] + jnp.dot(x, wg_ref[rows, :], preferred_element_type=f32),
                acc[1] + jnp.dot(x, wu_ref[rows, :], preferred_element_type=f32))
    zero = jnp.zeros((CAP, 768), f32)
    gate, up = lax.fori_loop(0, 8, up_step, (zero, zero))
    hidden = (gate / (1.0 + jnp.exp(-gate)) * up).astype(bf16)

    def down_step(n, _):
        y = jnp.dot(hidden, wd_ref[:, pl.ds(pl.multiple_of(n * 512, 512), 512)], preferred_element_type=f32).astype(bf16)
        for q in range(4):
            eo_ref[n * 4 + q] = y[:, q * 128:(q + 1) * 128]
        return 0
    lax.fori_loop(0, 8, down_step, 0)
    send_all(4, lambda to: eo_ref.at[to], eogot_ref.at[ctx])
    eogot_ref[ctx] = eo_ref[ctx]
    wait_all(recv_sem, 4, eogot_ref, N_CTX - 1)
    outs = eogot_ref[...].reshape(N_CTX * CAP, 128)
    part = jnp.dot(wt_ref[0], outs, preferred_element_type=f32)
    part += jnp.dot(wt_ref[1], outs, preferred_element_type=f32) + jnp.dot(wt_ref[2], outs, preferred_element_type=f32)
    part_ref[...] = part.reshape(N_HEAD, 32, 128)
    send_heads(5, lambda to: part_ref.at[to], partgot_ref.at[head])
    partgot_ref[head] = part_ref[head]
    wait_all(recv_sem, 5, partgot_ref, N_HEAD - 1)
    mixture = (partgot_ref[0] + partgot_ref[1]) + (partgot_ref[2] + partgot_ref[3])
    own = res_ref[pl.ds(pl.multiple_of(head * 32, 32), 32), :]
    out_ref[...] = (own + mixture).astype(bf16)
    wait_all(send_sem, 0, msg_ref, N_CTX - 1)
    wait_all(send_sem, 1, att_ref, N_CTX - 1)
    wait_all(send_sem, 2, zsum_ref, N_HEAD - 1)
    wait_all(send_sem, 3, take_ref, N_CTX - 1)
    wait_all(send_sem, 4, eo_ref, N_CTX - 1)
    wait_all(send_sem, 5, part_ref, N_HEAD - 1)


def rest(message, resid, w_out, routes, route_weights, w_gate, w_up, w_down):
    vm = pl.BlockSpec(memory_space=pltpu.VMEM)
    hbm = pl.BlockSpec(memory_space=pl.ANY)
    V = pltpu.VMEM
    return pl.pallas_call(
        rest_kernel,
        in_specs=[vm, vm, hbm, vm, vm, hbm, hbm, hbm],
        out_specs=vm,
        out_shape=jax.ShapeDtypeStruct((32, 128), bf16),
        scratch_shapes=[
            V((2048, 128), bf16), V((4096, 768), bf16), V((4096, 768), bf16), V((768, 4096), bf16),
            V((N_CTX, 80, 128), bf16), V((N_CTX, 64, 128), bf16), V((N_HEAD, ROWS, 128), f32),
            V((N_CTX, CAP, 128), bf16), V((N_CTX, CAP, 128), bf16), V((8, CAP, 512), bf16),
            V((N_CTX, CAP, 128), bf16), V((N_CTX, CAP, 128), bf16), V((N_HEAD, 32, 128), f32), V((N_HEAD, 32, 128), f32),
            V((ROWS, ROWS), f32), V((N_CTX * CAP, 128), bf16), V((N_CTX * CAP, 128), f32), V((3, ROWS, N_CTX * CAP), bf16),
            V((ROWS, 128), f32),
            pltpu.SemaphoreType.DMA((4,)), pltpu.SemaphoreType.DMA((6,)), pltpu.SemaphoreType.DMA((6,)),
        ],
        compiler_params=pltpu.CompilerParams(vmem_limit_bytes=48 << 20, collective_id=0, has_side_effects=True),
    )(message, resid, w_out, routes, route_weights, w_gate, w_up, w_down)


def on_device(queries, key_codes, value_codes, key_book, value_book, lengths, resid, w_out, norm_gain,
              routes, route_weights, w_gate, w_up, w_down):
    message = attend(queries, key_codes, value_codes, key_book, value_book, lengths, norm_gain)
    return rest(message, resid, w_out, routes, route_weights, w_gate, w_up, w_down)


def solution(mesh):
    return jax.shard_map(
        on_device,
        mesh=mesh,
        in_specs=(
            P(None, "head", None),
            P("head", None, None, "ctx"),
            P("head", None, None, "ctx"),
            P("head", None, None, None),
            P("head", None, None, None),
            P(),
            P(None, "ctx"),
            P("head", None, "ctx"),
            P("ctx"),
            P(),
            P(),
            P(("ctx", "head"), None, None),
            P(("ctx", "head"), None, None),
            P(("ctx", "head"), None, None),
        ),
        out_specs=P("head", "ctx"),
        check_vma=False,
    )
```

time: 1520 us -> 122 us (0.08)
  waiting for transfers between devices: 713 us -> 0 us
  matrix products: 413 us -> 0 us
  blocking collectives: 313 us -> 0 us
  Pallas kernels: 0 us -> 116 us
  local copies, waits for them, and re-layouts: 45.9 us -> 5.59 us
    reduce_scatter x1 -> x0, waiting for transfers between devices: 631 us -> none  [on_device(): lax.psum_scatter(spread.reshape(ctx_count * head_axis * share_rows, share...]
    dot_general x69 -> x0, matrix products: 413 us -> none  [the longest x32 379 us: dequantize(): jnp.einsum('scd,rsct->rsdt', codebook, onehot_codes, preferred_element_ty...]
    psum x2 -> x0, blocking collectives: 189 us -> none  [the longest x1 124 us: on_device(): lax.psum((totals * factors, outputs * factors[..., None]), 'ctx')]
    pmax x1 -> x0, blocking collectives: 124 us -> none  [on_device(): highest = lax.pmax(maxima, 'ctx')]
    pallas_call x0 -> x2, Pallas kernels: none -> 116 us  [the longest x1 62.7 us: attend(): pl.pallas_call(functools.partial(attn_kernel, unroll=unroll, SL=SL), in_s...]
    psum x2 -> x0, waiting for transfers between devices: 41.5 us -> none  [the longest x1 41.5 us: on_device(): projected = lax.psum(partial_proj, 'head')]
    all_gather x1 -> x0, waiting for transfers between devices: 40.4 us -> none  [on_device(): lax.all_gather(scaled.astype(jnp.bfloat16), 'ctx', axis=1, tiled=True)]
    dynamic_slice x64 -> x0, local copies, waits for them, and re-layouts: 36.1 us -> none  [on_device(): maxima, totals, outputs = lax.map(attend, packed)]
  transfers between devices with their start and end apart: 4 -> 0, of which waited for: 3 -> 0; matrix products, arithmetic and copies ran while one was open for 0% -> 0% of each run, Pallas kernels for 0% -> 0%
where the time goes in v1:
time: 122 us
  Pallas kernels  116 us (95%)
  local copies, waits for them, and re-layouts  5.59 us (5%)
    pallas_call x1, Pallas kernels, attend(): pl.pallas_call(functools.partial(attn_kernel, unroll=unroll, SL=SL), in_s...  62.7 us
    pallas_call x1, Pallas kernels, rest(): pl.pallas_call(rest_kernel, in_specs=[vm, vm, hbm, vm, vm, hbm, hbm, hbm]...  53.6 us

profile of v1, /device:TPU:1, one launch (start us, length us, event | category | flops | bytes accessed | tf_op | source)
XLA Modules:
  0.0 121.9 jit_solution(1999225471143255740)
XLA Ops:
  0.0 0.0 copy-start.3
  0.0 0.0 copy-start.4
  0.0 0.0 copy-start.2
  0.0 0.0 copy-start.1
  0.0 1.6 %copy_bitcast_fusion = (bf16[16,8,256]{2,1,0:T(8,128)(2,1)}, bf16[16,8,256]{2,1,0:T(8,128)(2,1)}) fusion(bf16[1,8,256,16]{2,3,1,0:T(8,128)(2,1)} %param.18, bf16[1,8,256,16]{2,3,1,0:T(8,128)(2,1)} %param.17), kind=kLoop, calls=%fused_computation | loop fusion | bytes 262144 | tf_op jit(solution)/shard_map/transpose | solution.py:148
  1.6 2.1 %reshape.6.q_ref = bf16[2048,128]{1,0:T(8,128)(2,1)} reshape(bf16[128,1,2048]{2,0,1:T(8,128)(2,1)} %param.14) | data formatting | bytes 1048576 | tf_op jit(solution)/shard_map/reshape | solution.py:147
  3.7 62.7 %shard_map.136.msg_ref = bf16[32,80,128]{2,1,0:T(8,128)(2,1)} custom-call(s32[128]{0:T(128)} %len_ref.1, bf16[2048,128]{1,0:T(8,128)(2,1)} %reshape.6.q_ref, bf16[16,8,256]{2,1,0:T(8,128)(2,1)} %get-tuple-element.6.kb_ref, bf16[16,8,256]{2,1,0:T(8,128)(2,1)} %get-tuple-element.5.vb_ref, bf16[1,128]{1,0:T(2,128)(2,1)} %bitcast.11, ...), custom_call_target="tpu_custom_call" | custom-call | tf_op jit(solution)/shard_map/pallas_call | solution.py:135
  66.4 0.0 copy-done.3
  66.4 0.1 copy.17.routes_ref
  66.5 0.0 copy-done.4
  66.5 0.1 copy.18.rw_ref
  66.6 0.0 copy-done.2
  66.6 0.0 copy-done.1
  66.6 0.0 copy-start
  66.6 1.1 copy-done
  67.7 53.6 %shard_map.137 = bf16[32,128]{1,0:T(8,128)(2,1)S(1)} custom-call(bf16[32,80,128]{2,1,0:T(8,128)(2,1)S(1)} %copy-done, bf16[128,128]{1,0:T(8,128)(2,1)S(1)} %copy-done.2, bf16[1,2048,128]{2,1,0:T(8,128)(2,1)S(1)} %copy-done.1, s32[128,8]{1,0:T(8,128)S(1)} %copy.17.routes_ref, f32[128,8]{1,0:T(8,128)S(1)} %copy.18.rw_ref, bf16[1,4096,768]{2,1,0:T(8,128)(2,1)} %wg_hbm.1, ...), custom_call_target="tpu_custom_call" | custom-call | tf_op jit(solution)/shard_map/pallas_call | solution.py:316
  121.3 0.6 copy.22
Async XLA Ops:
  0.0 66.4 %copy-start.3 = (s32[128,8]{0,1:T(8,128)S(1)}, s32[128,8]{0,1:T(8,128)}, u32[]{:S(2)}) copy-start(s32[128,8]{0,1:T(8,128)} %param.23) | copy-start | bytes 12292
  0.0 66.5 %copy-start.4 = (f32[128,8]{0,1:T(8,128)S(1)}, f32[128,8]{0,1:T(8,128)}, u32[]{:S(2)}) copy-start(f32[128,8]{0,1:T(8,128)} %param.24) | copy-start | bytes 12292
  0.0 66.6 %copy-start.2 = (bf16[128,128]{1,0:T(8,128)(2,1)S(1)}, bf16[128,128]{1,0:T(8,128)(2,1)}, u32[]{:S(2)}) copy-start(bf16[128,128]{1,0:T(8,128)(2,1)} %resid_ref.1) | copy-start | bytes 98308
  0.0 66.6 %copy-start.1 = (bf16[1,2048,128]{2,1,0:T(8,128)(2,1)S(1)}, bf16[1,2048,128]{2,1,0:T(8,128)(2,1)}, u32[]{:S(2)}) copy-start(bf16[1,2048,128]{2,1,0:T(8,128)(2,1)} %wout_hbm.1) | copy-start | bytes 1572868
  66.6 1.1 copy-start

commit v2 on v1

v2 whole, which is shorter than its diff:
```python
import functools, math
import jax, jax.numpy as jnp
from jax import lax
from jax.experimental import pallas as pl
from jax.experimental.pallas import tpu as pltpu
from jax.sharding import PartitionSpec as P
LOG2E = 1.4426950408889634
f32, bf16, i32 = jnp.float32, jnp.bfloat16, jnp.int32
ROWS, CH, CAP, N_CTX, N_HEAD = 128, 16, 16, 32, 4
UNROLL, SLOTS, AHEAD = 8, 4, 2
MESH = pl.DeviceIdType.MESH

def pow2_scale(x):
    sc = jnp.ones_like(x)
    for p in (32, 16, 8, 4, 2, 1):
        f = float(2.0 ** p)
        ok = x * f <= 4.0
        x = jnp.where(ok, x * f, x)
        sc = jnp.where(ok, sc * f, sc)
    return sc

def build_table(book_ref, table_ref):
    top = jnp.zeros((8, 256), f32)
    for d in range(16):
        top = jnp.maximum(top, jnp.abs(book_ref[d].astype(f32)))
    sc = pow2_scale(jnp.max(top, axis=1, keepdims=True))
    for p in range(8):
        hi = jnp.round(book_ref[2 * p].astype(f32) * (sc * 4096.0)).astype(i32)
        lo = jnp.round(book_ref[2 * p + 1].astype(f32) * (sc * 4096.0)).astype(i32)
        word = hi * 65536 + lo
        table_ref[2 * p] = word[:, :128]
        table_ref[2 * p + 1] = word[:, 128:]
    inv = 1.0 / sc * (2.0 ** -28)
    lane = lax.broadcasted_iota(i32, (8, 128), 1)
    sub = lax.broadcasted_iota(i32, (8, 128), 0)
    return jnp.sum(jnp.where(lane % 8 == sub, inv, 0.0), axis=0, keepdims=True)

def layer_kernel(len_ref, q_ref, kb_ref, vb_ref, gain_ref, resid_ref, routes_ref, rw_ref,
                 kc_hbm, vc_hbm, wout_hbm, wg_hbm, wu_hbm, wd_hbm,
                 out_ref,
                 kc_ref, vc_ref, kt_ref, vt_ref, qp_ref, ox_ref, key_ref, val_ref, ml_ref, swap_ref, msg_ref,
                 wout_ref, wg_ref, wu_ref, wd_ref, got_ref, att_ref, zsum_ref, take_ref, taken_ref, xn_ref,
                 eo_ref, eogot_ref, part_ref, partgot_ref, gt_ref, sel_ref, selw_ref, wt_ref, res_ref,
                 ksem, vsem, load_sem, send_sem, recv_sem):
    ctx = lax.axis_index("ctx")
    head = lax.axis_index("head")
    core = lax.rem(ctx, 2)
    chip = ctx // 2
    barrier = pltpu.get_barrier_semaphore()

    def greet_ctx(k, _):
        pl.semaphore_signal(barrier, inc=1, device_id={"ctx": lax.rem(ctx + k, N_CTX)}, device_id_type=MESH)
        return 0
    lax.fori_loop(1, N_CTX, greet_ctx, 0)
    for k in range(1, N_HEAD):
        pl.semaphore_signal(barrier, inc=1, device_id={"head": lax.rem(head + k, N_HEAD)}, device_id_type=MESH)

    def code_copy(c, hbm, vmem, sem):
        at = pl.ds(c * CH, CH)
        return pltpu.make_async_copy(hbm.at[0, at], vmem.at[at], sem.at[c])
    for c in range(ROWS // CH):
        code_copy(c, kc_hbm, kc_ref, ksem).start()
        code_copy(c, vc_hbm, vc_ref, vsem).start()
    loads = [pltpu.make_async_copy(wout_hbm.at[0], wout_ref, load_sem.at[0]),
             pltpu.make_async_copy(wg_hbm.at[0], wg_ref, load_sem.at[1]),
             pltpu.make_async_copy(wu_hbm.at[0], wu_ref, load_sem.at[2]),
             pltpu.make_async_copy(wd_hbm.at[0], wd_ref, load_sem.at[3])]
    for load in loads:
        load.start()

    offset = ctx * 1024
    k_inv = build_table(kb_ref, kt_ref)
    v_inv = build_table(vb_ref, vt_ref)
    i = lax.broadcasted_iota(i32, (128, 128), 0)
    j = lax.broadcasted_iota(i32, (128, 128), 1)
    to_ds = (i // 16 == j % 8) & (i % 16 == j // 8)
    to_sd = (j // 16 == i % 8) & (j % 16 == i // 8)
    perm = jnp.where(to_sd, 1.0, 0.0).astype(bf16)
    qp_ref[...] = jnp.dot(q_ref[...], jnp.where(to_ds, k_inv, 0.0).astype(bf16), preferred_element_type=f32).astype(bf16)
    ml_ref[...] = jnp.zeros_like(ml_ref)
    ox_ref[...] = jnp.zeros_like(ox_ref)
    r = lax.broadcasted_iota(i32, (256, 256), 0)
    c = lax.broadcasted_iota(i32, (256, 256), 1)
    swap_ref[...] = ((r // 16 == c % 16) & (r % 16 == c // 16)).astype(f32).astype(bf16)
    lane = lax.broadcasted_iota(i32, (16, 128), 1)
    pos = lax.broadcasted_iota(i32, (16, 1024), 1)
    C = 1.0 / math.sqrt(128.0)

    def three(x):
        hi = x.astype(bf16)
        rest = x - hi.astype(f32)
        mid = rest.astype(bf16)
        return hi, mid, (rest - mid.astype(f32)).astype(bf16)

    def dequant(codes_ref, b, table_ref, dst_ref, slot):
        for j in range(8):
            at = slice(j * 128, (j + 1) * 128)
            idx = codes_ref[b, :, at]
            low = idx & 127
            upper = idx > 127
            for p in range(8):
                w0 = jnp.take_along_axis(table_ref[2 * p], low, axis=1, mode="promise_in_bounds")
                w1 = jnp.take_along_axis(table_ref[2 * p + 1], low, axis=1, mode="promise_in_bounds")
                w = jnp.where(upper, w1, w0)
                pair = jnp.concatenate([w.astype(f32), (w << 16).astype(f32)], axis=0)
                dst_ref[slot, p * 16:(p + 1) * 16, at] = pair.astype(bf16)

    def fetch(b, slot):
        dequant(kc_ref, b, kt_ref, key_ref, slot)
        dequant(vc_ref, b, vt_ref, val_ref, slot)

    def row(b, slot):
        at = pl.ds(pl.multiple_of(b * 16, 16), 16)
        raw = jnp.dot(qp_ref[at, :], key_ref[slot], preferred_element_type=f32)
        vis = pos < len_ref[b] - offset
        raw = jnp.where(vis, raw, -1e30)
        top = raw[:, 0:128]
        for k in range(1, 8):
            top = jnp.maximum(top, raw[:, k * 128:(k + 1) * 128])
        top = jnp.max(top, axis=1, keepdims=True)
        w = jnp.where(vis, jnp.exp2((raw - top) * (C * LOG2E)), 0.0)
        tot = w[:, 0:128]
        for k in range(1, 8):
            tot = tot + w[:, k * 128:(k + 1) * 128]
        tot = jnp.dot(jnp.concatenate(three(tot), axis=1), jnp.ones((384, 128), bf16), preferred_element_type=f32)
        out = lax.dot_general(w.astype(bf16), val_ref[slot], (((1,), (1,)), ((), ())), preferred_element_type=f32)
        ox_ref[at, :] = (out * v_inv).astype(bf16)
        here = lane == b
        ml_ref[0] = jnp.where(here, top * C, ml_ref[0])
        ml_ref[1] = jnp.where(here, tot, ml_ref[1])

    def turn(c, part):
        y = jnp.dot(swap_ref[pl.ds(pl.multiple_of(part * 128, 128), 128), :],
                    ox_ref[pl.ds(pl.multiple_of(c * 256, 256), 256), :], preferred_element_type=f32).astype(bf16)
        y = jnp.dot(y, perm, preferred_element_type=f32).astype(bf16)
        at = pl.ds(pl.multiple_of(lax.rem(c, 4) * 16, 16), 16)
        for h in range(8):
            msg_ref[(part * 8 + h) * 2 + c // 4, at, :] = y[h * 16:(h + 1) * 16]

    def add_tail(half):
        pieces = [x.astype(f32) for x in three(ml_ref[0]) + three(ml_ref[1])]
        line = lax.broadcasted_iota(i32, (16, 128), 0)
        gain = jnp.where(line == 6, gain_ref[...].astype(f32), 0.0)
        for h in range(16):
            tail = gain
            for k in range(6):
                tail = jnp.where(line == k, pieces[k][h:h + 1, :], tail)
            msg_ref[2 * h + half, 64:80, :] = tail.astype(bf16)

    def remote(phase, src, dst, to):
        return pltpu.make_async_remote_copy(
            src_ref=src, dst_ref=dst, send_sem=send_sem.at[phase], recv_sem=recv_sem.at[phase],
            device_id=to, device_id_type=MESH)

    def send_quarter(q):
        half = q // 2
        rows = pl.ds(0, 32) if q % 2 == 0 else pl.ds(32, 48)

        def step(k, _):
            to = lax.rem(chip + k, 16) * 2 + half
            @pl.when(to != ctx)
            def _():
                remote(0, msg_ref.at[to, rows], got_ref.at[ctx, rows], {"ctx": to}).start()
            return 0
        lax.fori_loop(0, 16, step, 0)

    def send_all(phase, source, target):
        def step(k, _):
            to = lax.rem(ctx + k, N_CTX)
            remote(phase, source(to), target, {"ctx": to}).start()
            return 0
        lax.fori_loop(1, N_CTX, step, 0)

    def wait_all(sems, phase, ref, count):
        view = ref.at[pl.ds(0, count)]
        pltpu.make_async_copy(view, view, sems.at[phase]).wait()

    def send_heads(phase, source, target):
        for k in range(1, N_HEAD):
            to = lax.rem(head + k, N_HEAD)
            remote(phase, source(to), target, {"head": to}).start()

    def wait_chunk(c):
        code_copy(c, kc_hbm, kc_ref, ksem).wait()
        code_copy(c, vc_hbm, vc_ref, vsem).wait()
    wait_chunk(0)
    for b in range(AHEAD):
        fetch(b, b)
    pl.semaphore_wait(barrier, N_CTX - 1 + N_HEAD - 1)

    def chunk(c, _):
        @pl.when(c < ROWS // CH - 1)
        def _():
            wait_chunk(c + 1)

        def body(i, _):
            b = c * CH + i * UNROLL
            turn(jnp.maximum(c - 1, 0), i)
            for u in range(UNROLL):
                fetch(jnp.minimum(b + u + AHEAD, ROWS - 1), (u + AHEAD) % SLOTS)
                row(b + u, u % SLOTS)
            return 0
        lax.fori_loop(0, CH // UNROLL, body, 0)
        for q in range(3):
            @pl.when(c == 2 * q + 2)
            def _():
                if q == 1:
                    add_tail(0)
                send_quarter(q)
        return 0
    lax.fori_loop(0, ROWS // CH, chunk, 0)
    turn(ROWS // CH - 1, 0)
    turn(ROWS // CH - 1, 1)
    add_tail(1)
    send_quarter(3)
    got_ref[ctx] = msg_ref[ctx]

    eye = (lax.broadcasted_iota(i32, (8, 8), 0) == lax.broadcasted_iota(i32, (8, 8), 1)).astype(f32).astype(bf16)
    flip = lambda x: lax.dot_general(eye, x, (((1,), (1,)), ((), ())), preferred_element_type=f32)
    names = flip(routes_ref[...].astype(f32).astype(bf16)).astype(i32)
    rw = rw_ref[...]
    rw_hi = rw.astype(bf16)
    rw_mid = (rw - rw_hi.astype(f32)).astype(bf16)
    rw_lo = (rw - rw_hi.astype(f32) - rw_mid.astype(f32)).astype(bf16)
    shares = flip(rw_hi) + flip(rw_mid) + flip(rw_lo)
    expert = lax.broadcasted_iota(i32, (N_CTX, ROWS), 0) * N_HEAD + head
    member = jnp.zeros((N_CTX, ROWS), f32)
    weight = jnp.zeros((N_CTX, ROWS), f32)
    for k in range(8):
        same = names[k:k + 1, :] == expert
        member = jnp.where(same, 1.0, member)
        weight = jnp.where(same, shares[k:k + 1, :], weight)
    before = (lax.broadcasted_iota(i32, (ROWS, ROWS), 0) < lax.broadcasted_iota(i32, (ROWS, ROWS), 1)).astype(f32).astype(bf16)
    slot = jnp.dot(member.astype(bf16), before, preferred_element_type=f32).astype(i32)
    slot = jnp.where(member > 0.5, slot, -1)
    slots = lax.broadcasted_iota(i32, (CAP, ROWS), 0)
    for e in range(N_CTX):
        hit = slot[e:e + 1, :] == slots
        sel_ref[e * CAP:(e + 1) * CAP, :] = jnp.where(hit, 1.0, 0.0).astype(bf16)
        selw_ref[e * CAP:(e + 1) * CAP, :] = jnp.where(hit, weight[e:e + 1, :], 0.0)
    for t in range(N_CTX * CAP // 128):
        block = selw_ref[t * 128:(t + 1) * 128, :].T
        hi = block.astype(bf16)
        rest = block - hi.astype(f32)
        mid = rest.astype(bf16)
        wt_ref[0, :, t * 128:(t + 1) * 128] = hi
        wt_ref[1, :, t * 128:(t + 1) * 128] = mid
        wt_ref[2, :, t * 128:(t + 1) * 128] = (rest - mid.astype(f32)).astype(bf16)

    wait_all(recv_sem, 0, got_ref, N_CTX - 1)
    tails = got_ref[:, 64:80, :].reshape(N_CTX * 16, 128)
    r = lax.broadcasted_iota(i32, (3 * N_CTX, N_CTX * 16), 0)
    c = lax.broadcasted_iota(i32, (3 * N_CTX, N_CTX * 16), 1)
    kind, at = r // N_CTX, c % 16
    wanted = (c // 16 == r % N_CTX) & (at // 3 == kind) & (at < 7)
    stats = jnp.dot(jnp.where(wanted, 1.0, 0.0).astype(bf16), tails, preferred_element_type=f32)
    maxima, totals, gain = stats[:N_CTX], stats[N_CTX:2 * N_CTX], stats[2 * N_CTX:]
    factor = jnp.exp(maxima - jnp.max(maxima, axis=0, keepdims=True))
    factor = factor / jnp.sum(factor * totals, axis=0, keepdims=True)
    gt_ref[...] = jnp.concatenate([factor, jnp.zeros((ROWS - N_CTX, ROWS), f32)], axis=0).T
    mine = gt_ref[pl.ds(pl.multiple_of(core * 64, 64), 64), :]
    total = jnp.zeros((64, 128), f32)
    for s in range(N_CTX):
        total += mine[:, s:s + 1] * got_ref[s, :64, :].astype(f32)
    att_ref[core, chip] = total.astype(bf16)
    mine = att_ref.at[core, chip]

    def share(k, _):
        remote(1, mine, mine, {"ctx": lax.rem(chip + k, 16) * 2 + core}).start()
        return 0
    lax.fori_loop(1, 16, share, 0)
    loads[0].wait()
    wait_all(recv_sem, 1, att_ref.at[core], 15)
    sibling = remote(2, att_ref.at[core], att_ref.at[core], {"ctx": ctx + 1 - 2 * core})
    sibling.start()

    def project(half):
        proj = jnp.zeros((64, 128), f32)
        for h in range(16):
            proj += jnp.dot(att_ref[half, h], wout_ref[h * 128:(h + 1) * 128, :], preferred_element_type=f32)
        zsum_ref[head, half] = proj
        send_heads(3, lambda to: zsum_ref.at[head, half], zsum_ref.at[head, half])
    project(core)
    sibling.wait()
    project(1 - core)
    wait_all(recv_sem, 3, zsum_ref, N_HEAD - 1)
    projected = (zsum_ref[0] + zsum_ref[1]) + (zsum_ref[2] + zsum_ref[3])
    residual = (resid_ref[...].astype(f32) + projected.reshape(ROWS, 128)).astype(bf16)
    res_ref[...] = residual.astype(f32)

    take_ref[...] = jnp.dot(sel_ref[...], residual, preferred_element_type=f32).astype(bf16).reshape(N_CTX, CAP, 128)
    send_all(4, lambda to: take_ref.at[to], taken_ref.at[ctx])
    taken_ref[ctx] = take_ref[ctx]
    loads[1].wait()
    loads[2].wait()
    loads[3].wait()
    wait_all(recv_sem, 4, taken_ref, N_CTX - 1)
    squares = jnp.zeros((CAP, 128), f32)
    for s in range(N_CTX):
        piece = taken_ref[s].astype(f32)
        squares += piece * piece
    scale = lax.rsqrt(jnp.sum(squares, axis=1, keepdims=True) * (1.0 / 4096) + 1e-6)
    for s in range(N_CTX):
        piece = taken_ref[s].astype(f32) * scale * gain[s:s + 1, :]
        xn_ref[s // 4, :, s % 4 * 128:s % 4 * 128 + 128] = piece.astype(bf16)

    def up_step(k, acc):
        rows = pl.ds(pl.multiple_of(k * 512, 512), 512)
        x = xn_ref[k]
        return (acc[0] + jnp.dot(x, wg_ref[rows, :], preferred_element_type=f32),
                acc[1] + jnp.dot(x, wu_ref[rows, :], preferred_element_type=f32))
    zero = jnp.zeros((CAP, 768), f32)
    gate, up = lax.fori_loop(0, 8, up_step, (zero, zero))
    hidden = (gate / (1.0 + jnp.exp(-gate)) * up).astype(bf16)

    def down_step(n, _):
        y = jnp.dot(hidden, wd_ref[:, pl.ds(pl.multiple_of(n * 512, 512), 512)], preferred_element_type=f32).astype(bf16)
        for q in range(4):
            eo_ref[n * 4 + q] = y[:, q * 128:(q + 1) * 128]
        return 0
    lax.fori_loop(0, 8, down_step, 0)
    send_all(5, lambda to: eo_ref.at[to], eogot_ref.at[ctx])
    eogot_ref[ctx] = eo_ref[ctx]
    wait_all(recv_sem, 5, eogot_ref, N_CTX - 1)
    outs = eogot_ref[...].reshape(N_CTX * CAP, 128)
    part = jnp.dot(wt_ref[0], outs, preferred_element_type=f32)
    part += jnp.dot(wt_ref[1], outs, preferred_element_type=f32) + jnp.dot(wt_ref[2], outs, preferred_element_type=f32)
    part_ref[...] = part.reshape(N_HEAD, 32, 128)
    send_heads(6, lambda to: part_ref.at[to], partgot_ref.at[head])
    partgot_ref[head] = part_ref[head]
    wait_all(recv_sem, 6, partgot_ref, N_HEAD - 1)
    mixture = (partgot_ref[0] + partgot_ref[1]) + (partgot_ref[2] + partgot_ref[3])
    own = res_ref[pl.ds(pl.multiple_of(head * 32, 32), 32), :]
    out_ref[...] = (own + mixture).astype(bf16)
    wait_all(send_sem, 0, msg_ref, N_CTX - 1)
    wait_all(send_sem, 1, att_ref.at[core], 15)
    wait_all(send_sem, 3, zsum_ref, N_HEAD - 1)
    wait_all(send_sem, 4, take_ref, N_CTX - 1)
    wait_all(send_sem, 5, eo_ref, N_CTX - 1)
    wait_all(send_sem, 6, part_ref, N_HEAD - 1)


def on_device(queries, key_codes, value_codes, key_book, value_book, lengths, resid, w_out, norm_gain,
              routes, route_weights, w_gate, w_up, w_down):
    vm = pl.BlockSpec(memory_space=pltpu.VMEM)
    hbm = pl.BlockSpec(memory_space=pl.ANY)
    V = pltpu.VMEM
    dma = pltpu.SemaphoreType.DMA
    return pl.pallas_call(
        layer_kernel,
        in_specs=[pl.BlockSpec(memory_space=pltpu.SMEM)] + [vm] * 7 + [hbm] * 6,
        out_specs=vm,
        out_shape=jax.ShapeDtypeStruct((32, 128), bf16),
        scratch_shapes=[
            V((ROWS, 8, 1024), i32), V((ROWS, 8, 1024), i32), V((16, 8, 128), i32), V((16, 8, 128), i32),
            V((2048, 128), bf16), V((2048, 128), bf16), V((SLOTS, 128, 1024), bf16), V((SLOTS, 128, 1024), bf16),
            V((2, 16, 128), f32), V((256, 256), bf16), V((N_CTX, 80, 128), bf16),
            V((2048, 128), bf16), V((4096, 768), bf16), V((4096, 768), bf16), V((768, 4096), bf16),
            V((N_CTX, 80, 128), bf16), V((2, 16, 64, 128), bf16), V((N_HEAD, 2, 64, 128), f32),
            V((N_CTX, CAP, 128), bf16), V((N_CTX, CAP, 128), bf16), V((8, CAP, 512), bf16),
            V((N_CTX, CAP, 128), bf16), V((N_CTX, CAP, 128), bf16), V((N_HEAD, 32, 128), f32), V((N_HEAD, 32, 128), f32),
            V((ROWS, ROWS), f32), V((N_CTX * CAP, 128), bf16), V((N_CTX * CAP, 128), f32), V((3, ROWS, N_CTX * CAP), bf16),
            V((ROWS, 128), f32),
            dma((8,)), dma((8,)), dma((4,)), dma((7,)), dma((7,)),
        ],
        compiler_params=pltpu.CompilerParams(vmem_limit_bytes=58 << 20, collective_id=0, has_side_effects=True),
    )(lengths, queries.reshape(2048, 128), jnp.transpose(key_book[0], (2, 0, 1)),
      jnp.transpose(value_book[0], (2, 0, 1)), norm_gain.reshape(1, 128), resid, routes, route_weights,
      key_codes, value_codes, w_out, w_gate, w_up, w_down)


def solution(mesh):
    return jax.shard_map(
        on_device,
        mesh=mesh,
        in_specs=(
            P(None, "head", None),
            P("head", None, None, "ctx"),
            P("head", None, None, "ctx"),
            P("head", None, None, None),
            P("head", None, None, None),
            P(),
            P(None, "ctx"),
            P("head", None, "ctx"),
            P("ctx"),
            P(),
            P(),
            P(("ctx", "head"), None, None),
            P(("ctx", "head"), None, None),
            P(("ctx", "head"), None, None),
        ),
        out_specs=P("head", "ctx"),
        check_vma=False,
    )
```

time: 122 us -> 103 us (0.84)
  Pallas kernels: 116 us -> 95 us
  local copies, waits for them, and re-layouts: 5.59 us -> 7.74 us
    pallas_call x2 -> x1, Pallas kernels: 116 us -> 95 us  [on_device(): pl.pallas_call(layer_kernel, in_specs=[pl.BlockSpec(memory_space=pltpu.SM...]
    unnamed x13 -> x3, local copies, waits for them, and re-layouts: 1.9 us -> 4.11 us
where the time goes in v2:
time: 103 us
  Pallas kernels  95 us (92%)
  local copies, waits for them, and re-layouts  7.74 us (8%)
    pallas_call x1, Pallas kernels, on_device(): pl.pallas_call(layer_kernel, in_specs=[pl.BlockSpec(memory_space=pltpu.SM...  95 us
    unnamed x3, local copies, waits for them, and re-layouts  4.11 us
    reshape x1, local copies, waits for them, and re-layouts, on_device(): queries.reshape(2048, 128)  2.07 us

profile of v2, /device:TPU:1, one launch (start us, length us, event | category | flops | bytes accessed | tf_op | source)
XLA Modules:
  0.0 102.8 jit_solution(11749736422935243072)
XLA Ops:
  0.0 1.4 %copy.17.routes_ref = s32[128,8]{1,0:T(8,128)} copy(s32[128,8]{0,1:T(8,128)} %param.23) | data formatting | bytes 8192 | tf_op args[9]
  1.4 1.4 %copy.18.rw_ref = f32[128,8]{1,0:T(8,128)} copy(f32[128,8]{0,1:T(8,128)} %param.24) | data formatting | bytes 8192 | tf_op args[10]
  2.8 1.6 %copy_bitcast_fusion = (bf16[16,8,256]{2,1,0:T(8,128)(2,1)}, bf16[16,8,256]{2,1,0:T(8,128)(2,1)}) fusion(bf16[1,8,256,16]{2,3,1,0:T(8,128)(2,1)} %param.18, bf16[1,8,256,16]{2,3,1,0:T(8,128)(2,1)} %param.17), kind=kLoop, calls=%fused_computation | loop fusion | bytes 262144 | tf_op jit(solution)/shard_map/transpose | solution.py:368
  4.4 2.1 %reshape.6.q_ref = bf16[2048,128]{1,0:T(8,128)(2,1)} reshape(bf16[128,1,2048]{2,0,1:T(8,128)(2,1)} %param.14) | data formatting | bytes 1048576 | tf_op jit(solution)/shard_map/reshape | solution.py:367
  6.4 95.0 %shard_map.136 = bf16[32,128]{1,0:T(8,128)(2,1)} custom-call(s32[128]{0:T(128)} %len_ref.1, bf16[2048,128]{1,0:T(8,128)(2,1)} %reshape.6.q_ref, bf16[16,8,256]{2,1,0:T(8,128)(2,1)} %get-tuple-element.6.kb_ref, bf16[16,8,256]{2,1,0:T(8,128)(2,1)} %get-tuple-element.5.vb_ref, bf16[1,128]{1,0:T(2,128)(2,1)} %bitcast.11, bf16[128,128]{1,0:T(8,128)(2,1)} %resid_ref.1, ...), custom_call_target="tpu_custom_call" | custom-call | tf_op jit(solution)/shard_map/pallas_call | solution.py:349
  101.5 1.3 %copy.22 = bf16[32,128]{1,0:T(8,128)(2,1)} copy(bf16[32,128]{1,0:T(8,128)(2,1)} %shard_map.136) | data formatting | bytes 16384

commit v3 on v2

--- a/solution.py
+++ b/solution.py
@@ -19,14 +19,16 @@
         sc = jnp.where(ok, sc * f, sc)
     return sc
 
-def build_table(book_ref, table_ref):
-    top = jnp.zeros((8, 256), f32)
-    for d in range(16):
-        top = jnp.maximum(top, jnp.abs(book_ref[d].astype(f32)))
+def build_table(book_ref, table_ref, turn):
+    rows = jnp.dot(turn, book_ref[...].reshape(128, 256), preferred_element_type=f32)
+    entries = [rows[8 * d:8 * d + 8] for d in range(16)]
+    top = jnp.abs(entries[0])
+    for d in range(1, 16):
+        top = jnp.maximum(top, jnp.abs(entries[d]))
     sc = pow2_scale(jnp.max(top, axis=1, keepdims=True))
     for p in range(8):
-        hi = jnp.round(book_ref[2 * p].astype(f32) * (sc * 4096.0)).astype(i32)
-        lo = jnp.round(book_ref[2 * p + 1].astype(f32) * (sc * 4096.0)).astype(i32)
+        hi = jnp.round(entries[2 * p] * (sc * 4096.0)).astype(i32)
+        lo = jnp.round(entries[2 * p + 1] * (sc * 4096.0)).astype(i32)
         word = hi * 65536 + lo
         table_ref[2 * p] = word[:, :128]
         table_ref[2 * p + 1] = word[:, 128:]
@@ -69,19 +71,23 @@
         load.start()
 
     offset = ctx * 1024
-    k_inv = build_table(kb_ref, kt_ref)
-    v_inv = build_table(vb_ref, vt_ref)
     i = lax.broadcasted_iota(i32, (128, 128), 0)
     j = lax.broadcasted_iota(i32, (128, 128), 1)
     to_ds = (i // 16 == j % 8) & (i % 16 == j // 8)
     to_sd = (j // 16 == i % 8) & (j % 16 == i // 8)
     perm = jnp.where(to_sd, 1.0, 0.0).astype(bf16)
-    qp_ref[...] = jnp.dot(q_ref[...], jnp.where(to_ds, k_inv, 0.0).astype(bf16), preferred_element_type=f32).astype(bf16)
+    k_inv = build_table(kb_ref, kt_ref, perm)
+    v_inv = build_table(vb_ref, vt_ref, perm)
     ml_ref[...] = jnp.zeros_like(ml_ref)
     ox_ref[...] = jnp.zeros_like(ox_ref)
     r = lax.broadcasted_iota(i32, (256, 256), 0)
     c = lax.broadcasted_iota(i32, (256, 256), 1)
     swap_ref[...] = ((r // 16 == c % 16) & (r % 16 == c // 16)).astype(f32).astype(bf16)
+    k_perm = jnp.where(to_ds, k_inv, 0.0).astype(bf16)
+    for g in range(ROWS // CH):
+        x = jnp.concatenate([q_ref[g * CH:(g + 1) * CH, h * 128:(h + 1) * 128] for h in range(16)], axis=0)
+        x = jnp.dot(swap_ref[...], x, preferred_element_type=f32).astype(bf16)
+        qp_ref[g * 256:(g + 1) * 256, :] = jnp.dot(x, k_perm, preferred_element_type=f32).astype(bf16)
     lane = lax.broadcasted_iota(i32, (16, 128), 1)
     pos = lax.broadcasted_iota(i32, (16, 1024), 1)
     C = 1.0 / math.sqrt(128.0)
@@ -156,20 +162,19 @@
         half = q // 2
         rows = pl.ds(0, 32) if q % 2 == 0 else pl.ds(32, 48)
 
-        def step(k, _):
+        for k in range(1, 16):
             to = lax.rem(chip + k, 16) * 2 + half
-            @pl.when(to != ctx)
-            def _():
-                remote(0, msg_ref.at[to, rows], got_ref.at[ctx, rows], {"ctx": to}).start()
-            return 0
-        lax.fori_loop(0, 16, step, 0)
+            remote(0, msg_ref.at[to, rows], got_ref.at[ctx, rows], {"ctx": to}).start()
+
+        @pl.when(core != half)
+        def _():
+            to = chip * 2 + half
+            remote(0, msg_ref.at[to, rows], got_ref.at[ctx, rows], {"ctx": to}).start()
 
     def send_all(phase, source, target):
-        def step(k, _):
+        for k in range(1, N_CTX):
             to = lax.rem(ctx + k, N_CTX)
             remote(phase, source(to), target, {"ctx": to}).start()
-            return 0
-        lax.fori_loop(1, N_CTX, step, 0)
 
     def wait_all(sems, phase, ref, count):
         view = ref.at[pl.ds(0, count)]
@@ -215,14 +220,7 @@
     send_quarter(3)
     got_ref[ctx] = msg_ref[ctx]
 
-    eye = (lax.broadcasted_iota(i32, (8, 8), 0) == lax.broadcasted_iota(i32, (8, 8), 1)).astype(f32).astype(bf16)
-    flip = lambda x: lax.dot_general(eye, x, (((1,), (1,)), ((), ())), preferred_element_type=f32)
-    names = flip(routes_ref[...].astype(f32).astype(bf16)).astype(i32)
-    rw = rw_ref[...]
-    rw_hi = rw.astype(bf16)
-    rw_mid = (rw - rw_hi.astype(f32)).astype(bf16)
-    rw_lo = (rw - rw_hi.astype(f32) - rw_mid.astype(f32)).astype(bf16)
-    shares = flip(rw_hi) + flip(rw_mid) + flip(rw_lo)
+    names, shares = routes_ref[...], rw_ref[...]
     expert = lax.broadcasted_iota(i32, (N_CTX, ROWS), 0) * N_HEAD + head
     member = jnp.zeros((N_CTX, ROWS), f32)
     weight = jnp.zeros((N_CTX, ROWS), f32)
@@ -265,10 +263,8 @@
     att_ref[core, chip] = total.astype(bf16)
     mine = att_ref.at[core, chip]
 
-    def share(k, _):
+    for k in range(1, 16):
         remote(1, mine, mine, {"ctx": lax.rem(chip + k, 16) * 2 + core}).start()
-        return 0
-    lax.fori_loop(1, 16, share, 0)
     loads[0].wait()
     wait_all(recv_sem, 1, att_ref.at[core], 15)
     sibling = remote(2, att_ref.at[core], att_ref.at[core], {"ctx": ctx + 1 - 2 * core})
@@ -278,13 +274,14 @@
         proj = jnp.zeros((64, 128), f32)
         for h in range(16):
             proj += jnp.dot(att_ref[half, h], wout_ref[h * 128:(h + 1) * 128, :], preferred_element_type=f32)
-        zsum_ref[head, half] = proj
+        zsum_ref[head, half] = proj.astype(bf16)
         send_heads(3, lambda to: zsum_ref.at[head, half], zsum_ref.at[head, half])
     project(core)
     sibling.wait()
     project(1 - core)
     wait_all(recv_sem, 3, zsum_ref, N_HEAD - 1)
-    projected = (zsum_ref[0] + zsum_ref[1]) + (zsum_ref[2] + zsum_ref[3])
+    parts = [zsum_ref[z].astype(f32) for z in range(N_HEAD)]
+    projected = (parts[0] + parts[1]) + (parts[2] + parts[3])
     residual = (resid_ref[...].astype(f32) + projected.reshape(ROWS, 128)).astype(bf16)
     res_ref[...] = residual.astype(f32)
 
@@ -313,13 +310,18 @@
     gate, up = lax.fori_loop(0, 8, up_step, (zero, zero))
     hidden = (gate / (1.0 + jnp.exp(-gate)) * up).astype(bf16)
 
-    def down_step(n, _):
+    def down_step(k, _):
+        n = lax.rem(ctx // 4 + k, 8)
         y = jnp.dot(hidden, wd_ref[:, pl.ds(pl.multiple_of(n * 512, 512), 512)], preferred_element_type=f32).astype(bf16)
         for q in range(4):
-            eo_ref[n * 4 + q] = y[:, q * 128:(q + 1) * 128]
+            to = n * 4 + q
+            eo_ref[to] = y[:, q * 128:(q + 1) * 128]
+
+            @pl.when(to != ctx)
+            def _():
+                remote(5, eo_ref.at[to], eogot_ref.at[ctx], {"ctx": to}).start()
         return 0
     lax.fori_loop(0, 8, down_step, 0)
-    send_all(5, lambda to: eo_ref.at[to], eogot_ref.at[ctx])
     eogot_ref[ctx] = eo_ref[ctx]
     wait_all(recv_sem, 5, eogot_ref, N_CTX - 1)
     outs = eogot_ref[...].reshape(N_CTX * CAP, 128)
@@ -356,7 +358,7 @@
             V((2048, 128), bf16), V((2048, 128), bf16), V((SLOTS, 128, 1024), bf16), V((SLOTS, 128, 1024), bf16),
             V((2, 16, 128), f32), V((256, 256), bf16), V((N_CTX, 80, 128), bf16),
             V((2048, 128), bf16), V((4096, 768), bf16), V((4096, 768), bf16), V((768, 4096), bf16),
-            V((N_CTX, 80, 128), bf16), V((2, 16, 64, 128), bf16), V((N_HEAD, 2, 64, 128), f32),
+            V((N_CTX, 80, 128), bf16), V((2, 16, 64, 128), bf16), V((N_HEAD, 2, 64, 128), bf16),
             V((N_CTX, CAP, 128), bf16), V((N_CTX, CAP, 128), bf16), V((8, CAP, 512), bf16),
             V((N_CTX, CAP, 128), bf16), V((N_CTX, CAP, 128), bf16), V((N_HEAD, 32, 128), f32), V((N_HEAD, 32, 128), f32),
             V((ROWS, ROWS), f32), V((N_CTX * CAP, 128), bf16), V((N_CTX * CAP, 128), f32), V((3, ROWS, N_CTX * CAP), bf16),
@@ -364,8 +366,8 @@
             dma((8,)), dma((8,)), dma((4,)), dma((7,)), dma((7,)),
         ],
         compiler_params=pltpu.CompilerParams(vmem_limit_bytes=58 << 20, collective_id=0, has_side_effects=True),
-    )(lengths, queries.reshape(2048, 128), jnp.transpose(key_book[0], (2, 0, 1)),
-      jnp.transpose(value_book[0], (2, 0, 1)), norm_gain.reshape(1, 128), resid, routes, route_weights,
+    )(lengths, queries.reshape(ROWS, 2048), jnp.transpose(key_book[0], (0, 2, 1)),
+      jnp.transpose(value_book[0], (0, 2, 1)), norm_gain.reshape(1, 128), resid, routes.T, route_weights.T,
       key_codes, value_codes, w_out, w_gate, w_up, w_down)
 
 

time: 103 us -> 94.2 us (0.915)
  local copies, waits for them, and re-layouts: 7.74 us -> 1.3 us
  Pallas kernels: 95 us -> 92.7 us
    unnamed x3 -> x1, local copies, waits for them, and re-layouts: 4.11 us -> 1.3 us
    pallas_call x1, Pallas kernels: 95 us -> 92.7 us  [on_device(): pl.pallas_call(layer_kernel, in_specs=[pl.BlockSpec(memory_space=pltpu.SM...]
    reshape x1 -> x0, local copies, waits for them, and re-layouts: 2.07 us -> none  [on_device(): queries.reshape(2048, 128)]
    transpose x1 -> x0, local copies, waits for them, and re-layouts: 1.56 us -> none  [on_device(): jnp.transpose(value_book[0], (2, 0, 1))]
where the time goes in v3:
time: 94.2 us; the launch traced here: 94 us
  Pallas kernels  92.7 us (98%)
  local copies, waits for them, and re-layouts  1.3 us (1%)
    pallas_call x1, Pallas kernels, on_device(): pl.pallas_call(layer_kernel, in_specs=[pl.BlockSpec(memory_space=pltpu.SM...  92.7 us

profile of v3, /device:TPU:1, one launch (start us, length us, event | category | flops | bytes accessed | tf_op | source)
XLA Modules:
  0.0 94.0 jit_solution(5548074694293499129)
XLA Ops:
  0.0 92.7 %shard_map.136 = bf16[32,128]{1,0:T(8,128)(2,1)} custom-call(s32[128]{0:T(128)} %len_ref.1, bf16[128,2048]{1,0:T(8,128)(2,1)} %bitcast.10, bf16[8,16,256]{2,1,0:T(8,128)(2,1)} %bitcast.11, bf16[8,16,256]{2,1,0:T(8,128)(2,1)} %bitcast.12, bf16[1,128]{1,0:T(2,128)(2,1)} %bitcast.15, bf16[128,128]{1,0:T(8,128)(2,1)} %resid_ref.1, s32[8,128]{1,0:T(8,128)} %bitcast.13, ...), custom_call_target="tpu_custom_call" | custom-call | tf_op jit(solution)/shard_map/pallas_call | solution.py:351
  92.7 1.3 %copy.16 = bf16[32,128]{1,0:T(8,128)(2,1)} copy(bf16[32,128]{1,0:T(8,128)(2,1)} %shard_map.136) | data formatting | bytes 16384

commit v4 on v3

--- a/solution.py
+++ b/solution.py
@@ -7,7 +7,7 @@
 LOG2E = 1.4426950408889634
 f32, bf16, i32 = jnp.float32, jnp.bfloat16, jnp.int32
 ROWS, CH, CAP, N_CTX, N_HEAD = 128, 16, 16, 32, 4
-UNROLL, SLOTS, AHEAD = 8, 4, 2
+UNROLL, SLOTS, AHEAD = 16, 4, 2
 MESH = pl.DeviceIdType.MESH
 
 def pow2_scale(x):
@@ -84,10 +84,16 @@
     c = lax.broadcasted_iota(i32, (256, 256), 1)
     swap_ref[...] = ((r // 16 == c % 16) & (r % 16 == c // 16)).astype(f32).astype(bf16)
     k_perm = jnp.where(to_ds, k_inv, 0.0).astype(bf16)
-    for g in range(ROWS // CH):
-        x = jnp.concatenate([q_ref[g * CH:(g + 1) * CH, h * 128:(h + 1) * 128] for h in range(16)], axis=0)
-        x = jnp.dot(swap_ref[...], x, preferred_element_type=f32).astype(bf16)
-        qp_ref[g * 256:(g + 1) * 256, :] = jnp.dot(x, k_perm, preferred_element_type=f32).astype(bf16)
+
+    def turn_queries(c, part):
+        x = q_ref[pl.ds(pl.multiple_of(c * CH, CH), CH), :]
+        x = jnp.concatenate([x[:, h * 128:(h + 1) * 128] for h in range(16)], axis=0)
+        half = pl.multiple_of(part * 128, 128)
+        x = jnp.dot(swap_ref[pl.ds(half, 128), :], x, preferred_element_type=f32).astype(bf16)
+        at = pl.ds(pl.multiple_of(c * 256 + half, 128), 128)
+        qp_ref[at, :] = jnp.dot(x, k_perm, preferred_element_type=f32).astype(bf16)
+    turn_queries(0, 0)
+    turn_queries(0, 1)
     lane = lax.broadcasted_iota(i32, (16, 128), 1)
     pos = lax.broadcasted_iota(i32, (16, 1024), 1)
     C = 1.0 / math.sqrt(128.0)
@@ -123,7 +129,7 @@
         top = raw[:, 0:128]
         for k in range(1, 8):
             top = jnp.maximum(top, raw[:, k * 128:(k + 1) * 128])
-        top = jnp.max(top, axis=1, keepdims=True)
+        top = jnp.max(top.astype(bf16), axis=1, keepdims=True).astype(f32)
         w = jnp.where(vis, jnp.exp2((raw - top) * (C * LOG2E)), 0.0)
         tot = w[:, 0:128]
         for k in range(1, 8):
@@ -200,7 +206,9 @@
 
         def body(i, _):
             b = c * CH + i * UNROLL
-            turn(jnp.maximum(c - 1, 0), i)
+            for part in range(2) if UNROLL == CH else (i,):
+                turn(jnp.maximum(c - 1, 0), part)
+                turn_queries(jnp.minimum(c + 1, ROWS // CH - 1), part)
             for u in range(UNROLL):
                 fetch(jnp.minimum(b + u + AHEAD, ROWS - 1), (u + AHEAD) % SLOTS)
                 row(b + u, u % SLOTS)
@@ -307,26 +315,29 @@
         return (acc[0] + jnp.dot(x, wg_ref[rows, :], preferred_element_type=f32),
                 acc[1] + jnp.dot(x, wu_ref[rows, :], preferred_element_type=f32))
     zero = jnp.zeros((CAP, 768), f32)
-    gate, up = lax.fori_loop(0, 8, up_step, (zero, zero))
+    gate, up = lax.fori_loop(0, 8, up_step, (zero, zero), unroll=4)
     hidden = (gate / (1.0 + jnp.exp(-gate)) * up).astype(bf16)
 
     def down_step(k, _):
-        n = lax.rem(ctx // 4 + k, 8)
-        y = jnp.dot(hidden, wd_ref[:, pl.ds(pl.multiple_of(n * 512, 512), 512)], preferred_element_type=f32).astype(bf16)
-        for q in range(4):
-            to = n * 4 + q
-            eo_ref[to] = y[:, q * 128:(q + 1) * 128]
-
-            @pl.when(to != ctx)
-            def _():
-                remote(5, eo_ref.at[to], eogot_ref.at[ctx], {"ctx": to}).start()
+        for u in range(2):
+            n = lax.rem(ctx // 4 + 2 * k + u, 8)
+            y = jnp.dot(hidden, wd_ref[:, pl.ds(pl.multiple_of(n * 512, 512), 512)], preferred_element_type=f32).astype(bf16)
+            for q in range(4):
+                eo_ref[n * 4 + q] = y[:, q * 128:(q + 1) * 128]
+        for u in range(2):
+            for q in range(4):
+                to = lax.rem(ctx // 4 + 2 * k + u, 8) * 4 + q
+
+                @pl.when(to != ctx)
+                def _():
+                    remote(5, eo_ref.at[to], eogot_ref.at[ctx], {"ctx": to}).start()
         return 0
-    lax.fori_loop(0, 8, down_step, 0)
+    lax.fori_loop(0, 4, down_step, 0)
     eogot_ref[ctx] = eo_ref[ctx]
     wait_all(recv_sem, 5, eogot_ref, N_CTX - 1)
     outs = eogot_ref[...].reshape(N_CTX * CAP, 128)
-    part = jnp.dot(wt_ref[0], outs, preferred_element_type=f32)
-    part += jnp.dot(wt_ref[1], outs, preferred_element_type=f32) + jnp.dot(wt_ref[2], outs, preferred_element_type=f32)
+    part = jnp.dot(wt_ref[...].reshape(3 * ROWS, N_CTX * CAP), outs, preferred_element_type=f32)
+    part = part[:ROWS] + (part[ROWS:2 * ROWS] + part[2 * ROWS:])
     part_ref[...] = part.reshape(N_HEAD, 32, 128)
     send_heads(6, lambda to: part_ref.at[to], partgot_ref.at[head])
     partgot_ref[head] = part_ref[head]

time: 94.2 us -> 90.3 us (0.959)
  Pallas kernels: 92.7 us -> 88.8 us
    pallas_call x1, Pallas kernels: 92.7 us -> 88.8 us  [on_device(): pl.pallas_call(layer_kernel, in_specs=[pl.BlockSpec(memory_space=pltpu.SM...]
where the time goes in v4:
time: 90.3 us; the launch traced here: 90.1 us
  Pallas kernels  88.8 us (98%)
  local copies, waits for them, and re-layouts  1.3 us (1%)
    pallas_call x1, Pallas kernels, on_device(): pl.pallas_call(layer_kernel, in_specs=[pl.BlockSpec(memory_space=pltpu.SM...  88.8 us

profile of v4, /device:TPU:1, one launch (start us, length us, event | category | flops | bytes accessed | tf_op | source)
XLA Modules:
  0.0 90.1 jit_solution(4012109829546111549)
XLA Ops:
  0.0 88.8 %shard_map.136 = bf16[32,128]{1,0:T(8,128)(2,1)} custom-call(s32[128]{0:T(128)} %len_ref.1, bf16[128,2048]{1,0:T(8,128)(2,1)} %bitcast.10, bf16[8,16,256]{2,1,0:T(8,128)(2,1)} %bitcast.11, bf16[8,16,256]{2,1,0:T(8,128)(2,1)} %bitcast.12, bf16[1,128]{1,0:T(2,128)(2,1)} %bitcast.15, bf16[128,128]{1,0:T(8,128)(2,1)} %resid_ref.1, s32[8,128]{1,0:T(8,128)} %bitcast.13, ...), custom_call_target="tpu_custom_call" | custom-call | tf_op jit(solution)/shard_map/pallas_call | solution.py:362
  88.8 1.3 %copy.16 = bf16[32,128]{1,0:T(8,128)(2,1)} copy(bf16[32,128]{1,0:T(8,128)(2,1)} %shard_map.136) | data formatting | bytes 16384

commit v5 on v4

--- a/solution.py
+++ b/solution.py
@@ -9,6 +9,15 @@
 ROWS, CH, CAP, N_CTX, N_HEAD = 128, 16, 16, 32, 4
 UNROLL, SLOTS, AHEAD = 16, 4, 2
 MESH = pl.DeviceIdType.MESH
+
+
+def hops(k):
+    return min(k // 4, 4 - k // 4) + min(k % 4, 4 - k % 4)
+
+
+CHIP_STEPS = sorted(range(1, 16), key=lambda k: (-hops(k), k))
+CTX_STEPS = sorted(range(1, N_CTX), key=lambda k: (-hops(k // 2), k))
+HEAD_STEPS = (2, 1, 3)
 
 def pow2_scale(x):
     sc = jnp.ones_like(x)
@@ -168,7 +177,7 @@
         half = q // 2
         rows = pl.ds(0, 32) if q % 2 == 0 else pl.ds(32, 48)
 
-        for k in range(1, 16):
+        for k in CHIP_STEPS:
             to = lax.rem(chip + k, 16) * 2 + half
             remote(0, msg_ref.at[to, rows], got_ref.at[ctx, rows], {"ctx": to}).start()
 
@@ -178,7 +187,7 @@
             remote(0, msg_ref.at[to, rows], got_ref.at[ctx, rows], {"ctx": to}).start()
 
     def send_all(phase, source, target):
-        for k in range(1, N_CTX):
+        for k in CTX_STEPS:
             to = lax.rem(ctx + k, N_CTX)
             remote(phase, source(to), target, {"ctx": to}).start()
 
@@ -187,7 +196,7 @@
         pltpu.make_async_copy(view, view, sems.at[phase]).wait()
 
     def send_heads(phase, source, target):
-        for k in range(1, N_HEAD):
+        for k in HEAD_STEPS:
             to = lax.rem(head + k, N_HEAD)
             remote(phase, source(to), target, {"head": to}).start()
 
@@ -271,7 +280,7 @@
     att_ref[core, chip] = total.astype(bf16)
     mine = att_ref.at[core, chip]
 
-    for k in range(1, 16):
+    for k in CHIP_STEPS:
         remote(1, mine, mine, {"ctx": lax.rem(chip + k, 16) * 2 + core}).start()
     loads[0].wait()
     wait_all(recv_sem, 1, att_ref.at[core], 15)
@@ -320,13 +329,13 @@
 
     def down_step(k, _):
         for u in range(2):
-            n = lax.rem(ctx // 4 + 2 * k + u, 8)
+            n = lax.rem(ctx // 4 + 3 + 2 * k + u, 8)
             y = jnp.dot(hidden, wd_ref[:, pl.ds(pl.multiple_of(n * 512, 512), 512)], preferred_element_type=f32).astype(bf16)
             for q in range(4):
                 eo_ref[n * 4 + q] = y[:, q * 128:(q + 1) * 128]
         for u in range(2):
             for q in range(4):
-                to = lax.rem(ctx // 4 + 2 * k + u, 8) * 4 + q
+                to = lax.rem(ctx // 4 + 3 + 2 * k + u, 8) * 4 + q
 
                 @pl.when(to != ctx)
                 def _():

time: 90.3 us -> 89.3 us (0.989)
  Pallas kernels: 88.8 us -> 87.8 us
    pallas_call x1, Pallas kernels: 88.8 us -> 87.8 us  [on_device(): pl.pallas_call(layer_kernel, in_specs=[pl.BlockSpec(memory_space=pltpu.SM...]
where the time goes in v5:
time: 89.3 us; the launch traced here: 89.1 us
  Pallas kernels  87.8 us (98%)
  local copies, waits for them, and re-layouts  1.3 us (1%)
    pallas_call x1, Pallas kernels, on_device(): pl.pallas_call(layer_kernel, in_specs=[pl.BlockSpec(memory_space=pltpu.SM...  87.8 us

profile of v5, /device:TPU:1, one launch (start us, length us, event | category | flops | bytes accessed | tf_op | source)
XLA Modules:
  0.0 89.1 jit_solution(14715423990440794748)
XLA Ops:
  0.0 87.8 %shard_map.136 = bf16[32,128]{1,0:T(8,128)(2,1)} custom-call(s32[128]{0:T(128)} %len_ref.1, bf16[128,2048]{1,0:T(8,128)(2,1)} %bitcast.10, bf16[8,16,256]{2,1,0:T(8,128)(2,1)} %bitcast.11, bf16[8,16,256]{2,1,0:T(8,128)(2,1)} %bitcast.12, bf16[1,128]{1,0:T(2,128)(2,1)} %bitcast.15, bf16[128,128]{1,0:T(8,128)(2,1)} %resid_ref.1, s32[8,128]{1,0:T(8,128)} %bitcast.13, ...), custom_call_target="tpu_custom_call" | custom-call | tf_op jit(solution)/shard_map/pallas_call | solution.py:371
  87.8 1.3 %copy.16 = bf16[32,128]{1,0:T(8,128)(2,1)} copy(bf16[32,128]{1,0:T(8,128)(2,1)} %shard_map.136) | data formatting | bytes 16384
